TPU v7x, 256 devices: a whole 4x4x8 slice. The times are simulated.
256 devices in a mesh: rep: 8 (over y, core), grp: 32 (over z, x).
Axes of the slice: x: 4, y: 4, z: 8, core: 2. Of those that a mesh axis runs over, the one named last changes fastest.
Arguments:
- amps: float32 [8, 1024, 32768], P(None, None, ('rep', 'grp')), may hold values from -0.125 to 0.125
- integrals: float32 [8, 32768, 512], P(None, 'rep', 'grp'), may hold values from -6 to 6
- residual_other: float32 [1024, 8, 512], P(('rep', 'grp')), may hold values from -6 to 6
- row_gap: float32 [1024, 8], P(('rep', 'grp')), may hold values from 0.5 to 4
- col_gap: float32 [8, 512], replicated, may hold values from 0.5 to 4
- row_count: int32 [8], replicated, may hold values from 1 to 1024, 6144 in all
- k_count: int32 [8], replicated, may hold values from 1 to 32768, 196608 in all
- col_count: int32 [8], replicated, may hold values from 1 to 512, 3072 in all
Outputs:
- update: float32 [1024, 8, 512], P(('rep', 'grp'))
Inputs may be any that keep to these rules, and one draw needn't show every extreme that they name: `row_count`: live rows of the irreps sum to 6144; one irrep has exactly 1024. `k_count`: live summed pairs of the irreps sum to 196608; one irrep has exactly 32768. `col_count`: live columns of the irreps sum to 3072; one irrep has exactly 512.
All inputs are finite; a program needn't handle non-finite values.
Results may differ from a plain program's by a relative error of at most 0.0003.
Values sent between devices are 32-bit elements; how exact they have to be, the bound alone decides.
A program may use at most 128 MiB of HBM per device.

v0:
```python
import jax
import jax.numpy as jnp
from jax import lax
from jax.sharding import PartitionSpec as P


def local(amps, integrals, residual_other, row_gap, col_gap, row_count, k_count, col_count):
    k_local = amps.shape[2]
    columns = lax.all_to_all(integrals, "grp", split_axis=1, concat_axis=2, tiled=True)
    position = lax.axis_index("rep") * lax.axis_size("grp") + lax.axis_index("grp")
    k_index = position * k_local + jnp.arange(k_local, dtype=jnp.int32)[None, :, None]
    columns = jnp.where(k_index < k_count[:, None, None], columns, 0.0)
    rows_here = residual_other.shape[0]
    first_row = position * rows_here
    cycle_sum = lax.psum_scatter(
        jnp.einsum(
            "smk,skn->msn",
            amps,
            columns,
            precision=lax.Precision.HIGHEST,
            preferred_element_type=jnp.float32,
        ),
        ("rep", "grp"),
        scatter_dimension=0,
        tiled=True,
    )
    row_index = first_row + jnp.arange(rows_here, dtype=jnp.int32)[:, None, None]
    col_index = jnp.arange(col_gap.shape[1], dtype=jnp.int32)[None, None, :]
    live_mask = (row_index < row_count[None, :, None]) & (col_index < col_count[None, :, None])
    denominator = row_gap[:, :, None] + col_gap[None, :, :]
    return jnp.where(live_mask, -(cycle_sum + residual_other) / denominator, 0.0)


def solution(mesh):
    return jax.shard_map(
        local,
        mesh=mesh,
        in_specs=(
            P(None, None, ("rep", "grp")),
            P(None, "rep", "grp"),
            P(("rep", "grp"), None, None),
            P(("rep", "grp"), None),
            P(),
            P(),
            P(),
            P(),
        ),
        out_specs=P(("rep", "grp"), None, None),
        check_vma=False,
    )
```

profile of v0, /device:TPU:0, one launch (start us, length us, event | category | flops | bytes accessed | tf_op | source)
XLA Modules:
  0.0 1454.9 jit_solution(9818312255629763736)
XLA Ops:
  6.5 9.6 copy.13
  16.1 13.0 reshape.98
  29.1 0.0 copy-start.6
  29.1 9.7 all-to-all-start
  38.8 0.2 reduce-scatter.2.cloned.1.call-start
  39.0 0.0 copy-done.6
  39.1 0.1 broadcast_compare_fusion
  39.1 49.8 %all-to-all-done = f32[32,1,16384]{2,1,0:T(1,128)S(1)} async-done(((f32[32,1,16384]{2,1,0:T(1,128)}), f32[32,1,16384]{2,1,0:T(1,128)S(1)}, u32[]{:S(2)}, u32[]{:S(2)}) %all-to-all-start) | async-done | bytes 2097184 | tf_op jit(solution)/shard_map/all_to_all | solution.py:9
  89.0 0.0 copy-start
  89.0 1.3 copy-done
  90.3 0.5 broadcast.71
  90.8 7.4 reduce
  98.2 8.2 reshape.99
  106.4 9.6 copy.14
  116.0 0.0 copy-start.1
  116.0 0.2 bitcast_select_fusion
  116.2 2.0 copy-done.1
  118.2 15.7 %convolution_bitcast_fusion = f32[1024,8,512]{0,2,1:T(8,128)} fusion(f32[8,128,512]{1,2,0:T(8,128)S(1)} %bitcast_select_fusion, f32[8,1024,128]{2,1,0:T(8,128)S(1)} %copy-done.1), kind=kOutput, calls=%fused_computation | convolution fusion | flops 6442450944 | bytes 23068672 | tf_op jit(solution)/shard_map/smk,skn->msn/dot_general | solution.py:16
  133.9 17.5 %copy.15 = f32[1024,8,512]{2,1,0:T(8,128)} copy(f32[1024,8,512]{0,2,1:T(8,128)} %convolution_bitcast_fusion) | data formatting | bytes 33554432 | tf_op jit(solution)/shard_map/smk,skn->msn/transpose | solution.py:16
  151.4 0.0 copy-start.7
  151.4 0.0 copy-start.5
  151.4 0.0 copy-start.2
  151.4 0.0 copy-start.3
  151.4 0.0 copy-start.4
  151.5 0.0 reduce-scatter.2.cloned.1.call-update
  151.5 0.6 copy-done.7
  152.1 0.1 broadcast_compare_fusion.1
  152.2 0.0 copy-done.5
  152.2 0.1 iota_compare_fusion
  152.2 1294.3 %reduce-scatter.2.cloned.1.call-done = f32[4,8,512]{2,1,0:T(8,128)} async-done(((f32[1024,8,512]{2,1,0:T(8,128)}), f32[4,8,512]{2,1,0:T(8,128)}) %reduce-scatter.2.cloned.1.call-update) | async-done | bytes 65552 | tf_op jit(solution)/shard_map/reduce_scatter | solution.py:15
  1446.5 0.0 copy-done.2
  1446.5 0.0 copy-done.3
  1446.5 0.0 copy-done.4
  1446.5 1.6 divide_select_fusion
  (2 shorter events, 0.0 us)
Async XLA Ops:
  29.1 10.0 copy-start.6
  29.1 59.9 %all-to-all-start = ((f32[32,1,16384]{2,1,0:T(1,128)}), f32[32,1,16384]{2,1,0:T(1,128)S(1)}, u32[]{:S(2)}, u32[]{:S(2)}) async-start(f32[32,1,16384]{2,1,0:T(1,128)} %reshape.98), calls=%async_computation | async-start | bytes 4194304 | tf_op jit(solution)/shard_map/all_to_all | solution.py:9
  38.8 1407.7 %reduce-scatter.2.cloned.1.call-start = ((), (), s32[]{:S(2)}) async-start(), calls=%async_computation.2 | async-start | bytes 16842752 | tf_op jit(solution)/shard_map/reduce_scatter | solution.py:15
  89.0 1.3 copy-start
  116.0 2.2 copy-start.1
  151.4 0.7 copy-start.7
  151.4 0.7 copy-start.5
  151.4 1295.1 %copy-start.2 = (f32[4,8,512]{2,1,0:T(8,128)S(1)}, f32[4,8,512]{2,1,0:T(8,128)}, u32[]{:S(2)}) copy-start(f32[4,8,512]{2,1,0:T(8,128)} %param.10) | copy-start | bytes 196612
  151.4 1295.1 %copy-start.3 = (f32[8,512]{1,0:T(8,128)S(1)}, f32[8,512]{1,0:T(8,128)}, u32[]{:S(2)}) copy-start(f32[8,512]{1,0:T(8,128)} %param.12) | copy-start | bytes 49156
  151.4 1295.1 %copy-start.4 = (f32[4,8]{1,0:T(4,128)S(1)}, f32[4,8]{1,0:T(4,128)}, u32[]{:S(2)}) copy-start(f32[4,8]{1,0:T(4,128)} %param.11) | copy-start | bytes 388
Sparse Core Ops, SparseCore 0:
  151.6 1294.8 reduce-scatter.1
where the time goes:
time: 1460 us; the launch traced here: 1450 us
  waiting for transfers between devices  1340 us (92%)
  local copies, waits for them, and re-layouts  62.3 us (4%)
  matrix products  15.7 us (1%)
    reduce_scatter x1, waiting for transfers between devices, local(): lax.psum_scatter(jnp.einsum('smk,skn->msn', amps, columns, precision=lax....  1290 us
    all_to_all x1, waiting for transfers between devices, local(): lax.all_to_all(integrals, 'grp', split_axis=1, concat_axis=2, tiled=True)  49.8 us
    unnamed x19, local copies, waits for them, and re-layouts  34.7 us
  transfers between devices with their start and end apart: 2, of which 2 were waited for; matrix products, arithmetic and copies ran while one was open for 0% of the time, Pallas kernels for 0%

commit v1 on v0

v1 whole, which is shorter than its diff:
```python
import functools

import jax
import jax.numpy as jnp
from jax import lax
from jax.experimental import pallas as pl
from jax.experimental.pallas import tpu as pltpu
from jax.sharding import PartitionSpec as P

MESH = pl.DeviceIdType.MESH
NY, NC, NZ, NX = 4, 2, 8, 4
GRP = NZ * NX
NIRR = 8
ROWS = 1024
COLS = 512
KB = 128
CB = COLS // GRP
R = 4
HALF = ROWS // NC
PC = 384
QC = COLS - PC
AHEAD = 3


def kernel(
    amps, ints, k_count, out,
    blocks, lhs, rhs, c_send, c_recv,
    py_d, py_1, py_2, px_d, px_1, px_2,
    qx_d, qx_1, qx_2, qy_d, qy_1, qy_2,
    f_even, z_send, z_recv,
    x_ssem, x_rsem, c_ssem, c_rsem, p_ssem, p_rsem, z_ssem, z_rsem,
):
    rep, grp = lax.axis_index("rep"), lax.axis_index("grp")
    y, c = rep // NC, rep % NC
    z, x = grp // NX, grp % NX
    first_k = (rep * GRP + grp) * KB

    def peer(d):
        return lax.rem(z + d // NX, NZ) * NX + lax.rem(x + lax.rem(d, NX), NX)

    sibling = (y * NC + 1 - c, grp)

    def y_next(sign):
        return (lax.rem(y + NY + sign, NY) * NC + c, grp)

    def x_next(sign):
        return (rep, z * NX + lax.rem(x + NX + sign, NX))

    def z_peer(d):
        return lax.rem(z + d, NZ)

    barrier = pltpu.get_barrier_semaphore()

    def greet(d, _):
        pl.semaphore_signal(barrier, inc=1, device_id=(rep, peer(d)), device_id_type=MESH)
        return 0

    lax.fori_loop(1, GRP, greet, 0)
    for other in (sibling, y_next(1), y_next(-1)):
        pl.semaphore_signal(barrier, inc=1, device_id=other, device_id_type=MESH)
    pl.semaphore_wait(barrier, GRP + 2)

    def own_block(s):
        return pltpu.make_async_copy(
            ints.at[s, :, pl.ds(pl.multiple_of(grp * KB, KB), KB)],
            blocks.at[s, pl.ds(pl.multiple_of(grp * CB, CB), CB)],
            x_rsem.at[s],
        )

    def exchange(s):
        own_block(s).start()

        def send(d, _):
            to = peer(d)
            pltpu.make_async_remote_copy(
                ints.at[s, :, pl.ds(pl.multiple_of(to * KB, KB), KB)],
                blocks.at[s, pl.ds(pl.multiple_of(grp * CB, CB), CB)],
                x_ssem.at[s],
                x_rsem.at[s],
                device_id=(rep, to),
                device_id_type=MESH,
            ).start()
            return 0

        lax.fori_loop(1, GRP, send, 0)

    for s in range(AHEAD):
        exchange(s)

    def copy_1(s, ph, d):
        data, one, _, _, me, nxt = phases[ph]
        return pltpu.make_async_remote_copy(
            data.at[s, lax.rem(me + 2, 4), d],
            one.at[s, d],
            p_ssem.at[s, ph * 4 + d],
            p_rsem.at[s, ph * 4 + d],
            device_id=nxt(1 - 2 * d),
            device_id_type=MESH,
        )

    def copy_2(s, ph, d, h):
        data, _, two, _, me, nxt = phases[ph]
        return pltpu.make_async_remote_copy(
            data.at[s, lax.rem(me + (1, 3)[d], 4), h],
            two.at[s, d, h],
            p_ssem.at[s, ph * 4 + 2 + d],
            p_rsem.at[s, ph * 4 + 2 + d],
            device_id=nxt(1 - 2 * d),
            device_id_type=MESH,
        )

    def both_2(s, ph, d):
        _, _, two, _, _, nxt = phases[ph]
        return pltpu.make_async_remote_copy(
            two.at[s, d],
            two.at[s, d],
            p_ssem.at[s, ph * 4 + 2 + d],
            p_rsem.at[s, ph * 4 + 2 + d],
            device_id=nxt(1 - 2 * d),
            device_id_type=MESH,
        )

    phases = (
        (py_d, py_1, py_2, 64, y, y_next),
        (px_d, px_1, px_2, 16, x, x_next),
        (qx_d, qx_1, qx_2, 64, x, x_next),
        (qy_d, qy_1, qy_2, 16, y, y_next),
    )

    def begin(s, ph):
        for d in (0, 1):
            copy_1(s, ph, d).start()
        for d in (0, 1):
            copy_2(s, ph, d, 1 - d).start()

    def middle(s, ph):
        data, one, _, _, me, _ = phases[ph]
        for d in (0, 1):
            copy_1(s, ph, d).wait_recv()
            at = lax.rem(me + (1, 3)[d], 4)
            data[s, at, d] = data[s, at, d] + one[s, d]
            copy_2(s, ph, d, d).start()

    def end(s, ph):
        data, _, two, rows, me, _ = phases[ph]
        for d in (0, 1):
            both_2(s, ph, d).wait_recv()
        return data[s, me] + two[s, 0] + two[s, 1]

    def core_copy(s):
        return pltpu.make_async_remote_copy(
            c_send.at[s], c_recv.at[s], c_ssem.at[s], c_rsem.at[s], device_id=sibling, device_id_type=MESH
        )

    def prepare(s):
        low = (lax.broadcasted_iota(jnp.int32, (128, KB), 0) % 8) < 4

        def block(i, _):
            yy, cc = i // NC, lax.rem(i, NC)
            a = amps[s, pl.ds(pl.multiple_of(i * 128, 128), 128)]
            shape = (NZ // 2, 2, NX // 2, 8, KB)
            down = pltpu.roll(a, 4, 0)
            up = pltpu.roll(a, 124, 0)
            a5, d5, u5, l5 = (v.reshape(shape) for v in (a, down, up, low))
            even = jnp.where(l5[:, 0], a5[:, 0], d5[:, 1])
            odd = jnp.where(l5[:, 0], u5[:, 0], a5[:, 1])
            rows = jnp.concatenate(
                [v[:, p].reshape(NZ * R, KB) for p in range(NX // 2) for v in (even, odd)], axis=0
            )
            hi = rows.astype(jnp.bfloat16)
            lo = (rows - hi.astype(jnp.float32)).astype(jnp.bfloat16)
            lhs[pl.ds(pl.multiple_of(cc * HALF + yy * 128, 128), 128)] = jnp.concatenate([hi, lo], axis=1)
            return 0

        lax.fori_loop(0, NY * NC, block, 0)

    def product(half):
        left = lhs[pl.ds(pl.multiple_of(half * HALF, HALF), HALF)]
        dims = (((1,), (1,)), ((), ()))
        return lax.dot_general(left, rhs[0], dims, preferred_element_type=jnp.float32) + lax.dot_general(
            left, rhs[1], dims, preferred_element_type=jnp.float32
        )

    def multiply(s):
        pltpu.make_async_copy(blocks.at[s], blocks.at[s], x_rsem.at[s]).wait()
        k_index = first_k + lax.broadcasted_iota(jnp.int32, (COLS, KB), 1)
        b = jnp.where(k_index < k_count[s], blocks[s], 0.0)
        hi = b.astype(jnp.bfloat16)
        lo = (b - hi.astype(jnp.float32)).astype(jnp.bfloat16)
        rhs[0] = jnp.concatenate([hi, hi], axis=1)
        rhs[1] = jnp.concatenate([lo, lo], axis=1)
        c_send[s] = product(1 - c)
        core_copy(s).start()
        mine = product(c)
        core_copy(s).wait_recv()
        total = mine + c_recv[s]
        py_d[s] = total[:, :PC].reshape(NY, 2, 64, PC)
        q = total[:, PC:].reshape(NY, NX, NZ * R, QC)
        for xx in range(NX):
            qx_d[s, xx] = q[:, xx].reshape(2, 64, QC)
        begin(s, 0)
        begin(s, 2)

    def second(s):
        px_d[s] = end(s, 0).reshape(NX, 2, 16, PC)
        begin(s, 1)
        qy_d[s] = end(s, 2).reshape(NY, 2, 16, QC)
        begin(s, 3)

    def z_copy(p, d):
        to = z_peer(d)
        return pltpu.make_async_remote_copy(
            z_send.at[p, to],
            z_recv.at[p, z],
            z_ssem.at[p],
            z_rsem.at[p],
            device_id=(rep, to * NX + x),
            device_id_type=MESH,
        )

    def third(s):
        f = jnp.concatenate([end(s, 1).reshape(NZ * R, PC), end(s, 3).reshape(NZ * R, QC)], axis=1)

        @pl.when(lax.rem(s, 2) == 0)
        def _():
            f_even[...] = f

        @pl.when(lax.rem(s, 2) == 1)
        def _():
            p = s // 2
            e = f_even[...]
            low = (lax.broadcasted_iota(jnp.int32, f.shape, 0) % 8) < 4
            z_even = jnp.where(low, e, pltpu.roll(f, 4, 0)).reshape(NZ // 2, 8, COLS)
            z_odd = jnp.where(low, pltpu.roll(e, NZ * R - 4, 0), f).reshape(NZ // 2, 8, COLS)
            for i in range(NZ // 2):
                z_send[p, 2 * i] = z_even[i]
                z_send[p, 2 * i + 1] = z_odd[i]
            pltpu.make_async_copy(z_send.at[p, z], z_recv.at[p, z], z_rsem.at[p]).start()
            for d in range(1, NZ):
                z_copy(p, d).start()

    def step(t, _):
        @pl.when(t < NIRR)
        def _():
            prepare(t)

        @pl.when(t + AHEAD < NIRR)
        def _():
            exchange(t + AHEAD)

        @pl.when((t >= 1) & (t < NIRR + 1))
        def _():
            middle(t - 1, 0)
            middle(t - 1, 2)

        @pl.when(t >= 3)
        def _():
            third(t - 3)

        @pl.when((t >= 2) & (t < NIRR + 2))
        def _():
            second(t - 2)

        @pl.when(t < NIRR)
        def _():
            multiply(t)

        @pl.when((t >= 2) & (t < NIRR + 2))
        def _():
            middle(t - 2, 1)
            middle(t - 2, 3)

        return 0

    lax.fori_loop(0, NIRR + 3, step, 0)

    for p in range(NIRR // 2):
        pltpu.make_async_copy(z_recv.at[p], z_recv.at[p], z_rsem.at[p]).wait()
        total = z_recv[p, 0]
        for i in range(1, NZ):
            total = total + z_recv[p, i]
        out[p] = total

    def drain(s, _):
        most = blocks.at[s, pl.ds(0, COLS - CB)]
        pltpu.make_async_copy(most, most, x_ssem.at[s]).wait()
        core_copy(s).wait_send()
        for ph in range(4):
            for d in (0, 1):
                copy_1(s, ph, d).wait_send()
                both_2(s, ph, d).wait_send()
        return 0

    lax.fori_loop(0, NIRR, drain, 0)
    for p in range(NIRR // 2):
        most = z_send.at[p, pl.ds(0, NZ - 1)]
        pltpu.make_async_copy(most, most, z_ssem.at[p]).wait()


def cycle_of(amps, ints, k_count):
    f32 = jnp.float32
    return pl.pallas_call(
        kernel,
        out_shape=jax.ShapeDtypeStruct((NIRR // 2, 2 * R, COLS), f32),
        in_specs=[
            pl.BlockSpec(memory_space=pltpu.VMEM),
            pl.BlockSpec(memory_space=pl.ANY),
            pl.BlockSpec(memory_space=pltpu.SMEM),
        ],
        out_specs=pl.BlockSpec(memory_space=pltpu.VMEM),
        scratch_shapes=[
            pltpu.VMEM((NIRR, COLS, KB), f32),
            pltpu.VMEM((ROWS, 2 * KB), jnp.bfloat16),
            pltpu.VMEM((2, COLS, 2 * KB), jnp.bfloat16),
            pltpu.VMEM((NIRR, HALF, COLS), f32),
            pltpu.VMEM((NIRR, HALF, COLS), f32),
            pltpu.VMEM((NIRR, 4, 2, 64, PC), f32),
            pltpu.VMEM((NIRR, 2, 64, PC), f32),
            pltpu.VMEM((NIRR, 2, 2, 64, PC), f32),
            pltpu.VMEM((NIRR, 4, 2, 16, PC), f32),
            pltpu.VMEM((NIRR, 2, 16, PC), f32),
            pltpu.VMEM((NIRR, 2, 2, 16, PC), f32),
            pltpu.VMEM((NIRR, 4, 2, 64, QC), f32),
            pltpu.VMEM((NIRR, 2, 64, QC), f32),
            pltpu.VMEM((NIRR, 2, 2, 64, QC), f32),
            pltpu.VMEM((NIRR, 4, 2, 16, QC), f32),
            pltpu.VMEM((NIRR, 2, 16, QC), f32),
            pltpu.VMEM((NIRR, 2, 2, 16, QC), f32),
            pltpu.VMEM((NZ * R, COLS), f32),
            pltpu.VMEM((NIRR // 2, NZ, 2 * R, COLS), f32),
            pltpu.VMEM((NIRR // 2, NZ, 2 * R, COLS), f32),
            pltpu.SemaphoreType.DMA((NIRR,)),
            pltpu.SemaphoreType.DMA((NIRR,)),
            pltpu.SemaphoreType.DMA((NIRR,)),
            pltpu.SemaphoreType.DMA((NIRR,)),
            pltpu.SemaphoreType.DMA((NIRR, 16)),
            pltpu.SemaphoreType.DMA((NIRR, 16)),
            pltpu.SemaphoreType.DMA((NIRR // 2,)),
            pltpu.SemaphoreType.DMA((NIRR // 2,)),
        ],
        compiler_params=pltpu.CompilerParams(
            collective_id=0, has_side_effects=True, vmem_limit_bytes=56 * 2**20
        ),
        cost_estimate=pl.CostEstimate(
            flops=2 * NIRR * ROWS * COLS * KB * 4, bytes_accessed=6 * 2**20, transcendentals=0
        ),
    )(amps, ints, k_count)


def local(amps, integrals, residual_other, row_gap, col_gap, row_count, k_count, col_count):
    position = lax.axis_index("rep") * lax.axis_size("grp") + lax.axis_index("grp")
    rows_here = residual_other.shape[0]
    first_row = position * rows_here
    cycle = cycle_of(amps, jnp.swapaxes(integrals, 1, 2), k_count)
    cycle_sum = jnp.swapaxes(cycle.reshape(NIRR, R, COLS), 0, 1)
    row_index = first_row + jnp.arange(rows_here, dtype=jnp.int32)[:, None, None]
    col_index = jnp.arange(col_gap.shape[1], dtype=jnp.int32)[None, None, :]
    live_mask = (row_index < row_count[None, :, None]) & (col_index < col_count[None, :, None])
    denominator = row_gap[:, :, None] + col_gap[None, :, :]
    return jnp.where(live_mask, -(cycle_sum + residual_other) / denominator, 0.0)


def solution(mesh):
    return jax.shard_map(
        local,
        mesh=mesh,
        in_specs=(
            P(None, None, ("rep", "grp")),
            P(None, "rep", "grp"),
            P(("rep", "grp"), None, None),
            P(("rep", "grp"), None),
            P(),
            P(),
            P(),
            P(),
        ),
        out_specs=P(("rep", "grp"), None, None),
        check_vma=False,
    )
```

time: 1460 us -> 124 us (0.08)
  waiting for transfers between devices: 1340 us -> 0 us
  Pallas kernels: 0 us -> 119 us
  local copies, waits for them, and re-layouts: 62.3 us -> 0.87 us
  matrix products: 15.7 us -> 0 us
    reduce_scatter x1 -> x0, waiting for transfers between devices: 1290 us -> none  [local(): lax.psum_scatter(jnp.einsum('smk,skn->msn', amps, columns, precision=lax....]
    pallas_call x0 -> x1, Pallas kernels: none -> 119 us  [cycle_of(): pl.pallas_call(kernel, out_shape=jax.ShapeDtypeStruct((NIRR // 2, 2 * R,...]
    all_to_all x1 -> x0, waiting for transfers between devices: 49.8 us -> none  [local(): lax.all_to_all(integrals, 'grp', split_axis=1, concat_axis=2, tiled=True)]
    unnamed x19 -> x6, local copies, waits for them, and re-layouts: 34.7 us -> 0.01 us
    transpose x1 -> x0, local copies, waits for them, and re-layouts: 17.5 us -> none  [local(): jnp.einsum('smk,skn->msn', amps, columns, precision=lax.Precision.HIGHEST...]
    dot_general x1 -> x0, matrix products: 15.7 us -> none  [local(): jnp.einsum('smk,skn->msn', amps, columns, precision=lax.Precision.HIGHEST...]
  transfers between devices with their start and end apart: 2 -> 0, of which waited for: 2 -> 0; matrix products, arithmetic and copies ran while one was open for 0% -> 0% of each run, Pallas kernels for 0% -> 0%
where the time goes in v1:
time: 124 us; the launch traced here: 122 us
  Pallas kernels  119 us (96%)
  other arithmetic  2.17 us (2%)
    pallas_call x1, Pallas kernels, cycle_of(): pl.pallas_call(kernel, out_shape=jax.ShapeDtypeStruct((NIRR // 2, 2 * R,...  119 us

profile of v1, /device:TPU:0, one launch (start us, length us, event | category | flops | bytes accessed | tf_op | source)
XLA Modules:
  0.0 122.2 jit_solution(4684965634784311113)
XLA Ops:
  0.0 0.7 broadcast_compare_fusion
  0.7 0.7 iota_compare_fusion
  1.5 0.0 copy-start
  1.5 0.0 copy-start.1
  1.5 0.0 copy-start.2
  1.5 119.1 %shard_map.82 = f32[4,8,512]{2,1,0:T(8,128)} custom-call(f32[8,1024,128]{2,1,0:T(8,128)} %amps.1, f32[8,16,4096]{2,1,0:T(8,128)} %bitcast.9, s32[8]{0:T(128)} %k_count.1), custom_call_target="tpu_custom_call" | custom-call | flops 4294967296 | bytes 6291456 | tf_op jit(solution)/shard_map/pallas_call | solution.py:302
  120.5 0.9 reshape.63
  121.4 0.0 copy-done
  121.4 0.0 copy-done.1
  121.4 0.0 copy-done.2
  121.4 0.7 fusion.2
  (1 shorter events, 0.0 us)
Async XLA Ops:
  1.5 120.0 %copy-start = (f32[4,8,512]{2,1,0:T(8,128)S(1)}, f32[4,8,512]{2,1,0:T(8,128)}, u32[]{:S(2)}) copy-start(f32[4,8,512]{2,1,0:T(8,128)} %param.10) | copy-start | bytes 196612
  1.5 120.0 %copy-start.1 = (f32[8,512]{1,0:T(8,128)S(1)}, f32[8,512]{1,0:T(8,128)}, u32[]{:S(2)}) copy-start(f32[8,512]{1,0:T(8,128)} %param.12) | copy-start | bytes 49156
  1.5 120.0 %copy-start.2 = (f32[4,8]{1,0:T(4,128)S(1)}, f32[4,8]{1,0:T(4,128)}, u32[]{:S(2)}) copy-start(f32[4,8]{1,0:T(4,128)} %param.11) | copy-start | bytes 388

commit v2 on v1

v2 whole, which is shorter than its diff:
```python
import jax
import jax.numpy as jnp
from jax import lax
from jax.experimental import pallas as pl
from jax.experimental.pallas import tpu as pltpu
from jax.sharding import PartitionSpec as P

MESH = pl.DeviceIdType.MESH
NY, NC, NZ, NX = 4, 2, 8, 4
GRP = NZ * NX
NIRR = 8
ROWS = 1024
COLS = 512
KB = 128
R = 4
HALF = ROWS // NC
NST = 2 * NIRR
CB = 8
WIDE = GRP * CB
LANES = 128
UNITS = NZ * R * (WIDE // LANES)
PR = 40
QR = UNITS - PR
AHEAD = 6
LAG_M, LAG_S, LAG_T, LAG_Z = 2, 4, 6, 8


def kernel(
    amps, ints, residual, col_gap, row_gap, row_count, k_count, col_count, out,
    left, blocks, lhs, rhs, c_send, c_recv, c_mine,
    py_d, py_1, py_2, px_d, px_r,
    qx_d, qx_1, qx_2, qy_d, qy_r,
    f_even, z_send, z_recv, gaps, limits, cycle,
    a_sem, x_ssem, x_rsem, c_ssem, c_rsem, p_ssem, p_rsem, d_ssem, d_rsem, z_ssem, z_rsem,
):
    rep, grp = lax.axis_index("rep"), lax.axis_index("grp")
    y, c = rep // NC, rep % NC
    z, x = grp // NX, grp % NX
    first_k = (rep * GRP + grp) * KB

    def swing(j, n):
        step = (j + 1) // 2
        return lax.rem(n // 2 + n + (1 - 2 * lax.rem(j, 2)) * step, n)

    def peer(d):
        return lax.rem(z + swing(d // NX, NZ), NZ) * NX + lax.rem(x + swing(lax.rem(d, NX), NX), NX)

    sibling = (y * NC + 1 - c, grp)

    def y_next(sign):
        return (lax.rem(y + sign, NY) * NC + c, grp)

    def x_next(sign):
        return (rep, z * NX + lax.rem(x + sign, NX))

    def z_peer(d):
        return lax.rem(z + d, NZ)

    def load(s):
        return pltpu.make_async_copy(amps.at[s], left.at[s], a_sem.at[s])

    for s in range(NIRR):
        load(s).start()
    barrier = pltpu.get_barrier_semaphore()

    def greet(d, _):
        pl.semaphore_signal(barrier, inc=1, device_id=(rep, peer(d)), device_id_type=MESH)
        return 0

    lax.fori_loop(0, GRP - 1, greet, 0)
    for other in (sibling, y_next(1), y_next(2), y_next(3)):
        pl.semaphore_signal(barrier, inc=1, device_id=other, device_id_type=MESH)

    def own_block(s):
        return pltpu.make_async_copy(
            ints.at[s // 2, lax.rem(s, 2), :, pl.ds(pl.multiple_of(grp * KB, KB), KB)],
            blocks.at[s, pl.ds(pl.multiple_of(grp * CB, CB), CB)],
            x_rsem.at[s],
        )

    def exchange(s):
        own_block(s).start()

        def send(d, _):
            to = peer(d)
            pltpu.make_async_remote_copy(
                ints.at[s // 2, lax.rem(s, 2), :, pl.ds(pl.multiple_of(to * KB, KB), KB)],
                blocks.at[s, pl.ds(pl.multiple_of(grp * CB, CB), CB)],
                x_ssem.at[s],
                x_rsem.at[s],
                device_id=(rep, to),
                device_id_type=MESH,
            ).start()
            return 0

        lax.fori_loop(0, GRP - 1, send, 0)

    def copy_1(s, ph, d):
        data, one, _, me, nxt = phases[ph]
        return pltpu.make_async_remote_copy(
            data.at[s, lax.rem(me + 2, 4), d],
            one.at[s, d],
            p_ssem.at[s, ph * 4 + d],
            p_rsem.at[s, ph * 4 + d],
            device_id=nxt(1 + 2 * d),
            device_id_type=MESH,
        )

    def copy_2(s, ph, d, h):
        data, _, two, me, nxt = phases[ph]
        return pltpu.make_async_remote_copy(
            data.at[s, lax.rem(me + (1, 3)[d], 4), h],
            two.at[s, d, h],
            p_ssem.at[s, ph * 4 + 2 + d],
            p_rsem.at[s, ph * 4 + 2 + d],
            device_id=nxt(1 + 2 * d),
            device_id_type=MESH,
        )

    def both_2(s, ph, d):
        _, _, two, _, nxt = phases[ph]
        return pltpu.make_async_remote_copy(
            two.at[s, d],
            two.at[s, d],
            p_ssem.at[s, ph * 4 + 2 + d],
            p_rsem.at[s, ph * 4 + 2 + d],
            device_id=nxt(1 + 2 * d),
            device_id_type=MESH,
        )

    phases = (
        (py_d, py_1, py_2, y, y_next),
        (qx_d, qx_1, qx_2, x, x_next),
    )

    def begin(s, ph):
        for d in (0, 1):
            copy_1(s, ph, d).start()
        for d in (0, 1):
            copy_2(s, ph, d, 1 - d).start()

    def middle(s, ph):
        data, one, _, me, _ = phases[ph]
        for d in (0, 1):
            copy_1(s, ph, d).wait_recv()
            at = lax.rem(me + (1, 3)[d], 4)
            data[s, at, d] = data[s, at, d] + one[s, d]
            copy_2(s, ph, d, d).start()

    def end(s, ph):
        data, _, two, me, _ = phases[ph]
        for d in (0, 1):
            both_2(s, ph, d).wait_recv()
        return data[s, me] + two[s, 0] + two[s, 1]

    straight = ((px_d, px_r, x, x_next), (qy_d, qy_r, y, y_next))

    def copy_straight(s, ph, d):
        data, got, me, nxt = straight[ph]
        return pltpu.make_async_remote_copy(
            data.at[s, lax.rem(me + d, 4)],
            got.at[s, d - 1],
            d_ssem.at[s, ph * 3 + d - 1],
            d_rsem.at[s, ph * 3 + d - 1],
            device_id=nxt(d),
            device_id_type=MESH,
        )

    def begin_straight(s, ph):
        for d in (2, 1, 3):
            copy_straight(s, ph, d).start()

    def end_straight(s, ph):
        data, got, me, _ = straight[ph]
        for d in (1, 2, 3):
            copy_straight(s, ph, d).wait_recv()
        return data[s, me] + got[s, 0] + got[s, 1] + got[s, 2]

    def core_copy(s):
        return pltpu.make_async_remote_copy(
            c_send.at[s], c_recv.at[s], c_ssem.at[s], c_rsem.at[s], device_id=sibling, device_id_type=MESH
        )

    def prepare(s):
        load(s).wait()
        low = (lax.broadcasted_iota(jnp.int32, (128, KB), 0) % 8) < 4

        def block(i, _):
            yy, cc = i // NC, lax.rem(i, NC)
            a = left[s, pl.ds(pl.multiple_of(i * 128, 128), 128)]
            shape = (NZ // 2, 2, NX // 2, 8, KB)
            down = pltpu.roll(a, 4, 0)
            up = pltpu.roll(a, 124, 0)
            a5, d5, u5, l5 = (v.reshape(shape) for v in (a, down, up, low))
            even = jnp.where(l5[:, 0], a5[:, 0], d5[:, 1])
            odd = jnp.where(l5[:, 0], u5[:, 0], a5[:, 1])
            rows = jnp.concatenate(
                [v[:, p].reshape(NZ * R, KB) for p in range(NX // 2) for v in (even, odd)], axis=0
            )
            hi = rows.astype(jnp.bfloat16)
            lo = (rows - hi.astype(jnp.float32)).astype(jnp.bfloat16)
            lhs[pl.ds(pl.multiple_of(cc * HALF + yy * 128, 128), 128)] = jnp.concatenate([hi, lo], axis=1)
            return 0

        lax.fori_loop(0, NY * NC, block, 0)

    def product(half):
        rows = lhs[pl.ds(pl.multiple_of(half * HALF, HALF), HALF)]
        dims = (((1,), (1,)), ((), ()))
        return lax.dot_general(rows, rhs[0], dims, preferred_element_type=jnp.float32) + lax.dot_general(
            rows, rhs[1], dims, preferred_element_type=jnp.float32
        )

    def multiply(s):
        pltpu.make_async_copy(blocks.at[s], blocks.at[s], x_rsem.at[s]).wait()
        k_index = first_k + lax.broadcasted_iota(jnp.int32, (WIDE, KB), 1)
        b = jnp.where(k_index < k_count[s // 2], blocks[s], 0.0)
        hi = b.astype(jnp.bfloat16)
        lo = (b - hi.astype(jnp.float32)).astype(jnp.bfloat16)
        rhs[0] = jnp.concatenate([hi, hi], axis=1)
        rhs[1] = jnp.concatenate([lo, lo], axis=1)
        c_send[s] = product(1 - c)
        core_copy(s).start()
        c_mine[...] = product(c)

    def first(s):
        core_copy(s).wait_recv()
        total = (c_mine[...] + c_recv[s]).reshape(NY, NX, NZ * R, WIDE)
        total = jnp.concatenate([total[..., :LANES], total[..., LANES:]], axis=2)
        py_d[s] = total[:, :, :PR].reshape(NY, 2, NX * PR // 2, LANES)
        begin(s, 0)
        for xx in range(NX):
            qx_d[s, xx] = total[:, xx, PR:].reshape(2, NY * QR // 2, LANES)
        begin(s, 1)

    def second(s):
        px_d[s] = end(s, 0).reshape(NX, PR, LANES)
        begin_straight(s, 0)
        qy_d[s] = end(s, 1).reshape(NY, QR, LANES)
        begin_straight(s, 1)

    def z_copy(p, d):
        to = z_peer(d)
        return pltpu.make_async_remote_copy(
            z_send.at[p, to],
            z_recv.at[p, z],
            z_ssem.at[p],
            z_rsem.at[p],
            device_id=(rep, to * NX + x),
            device_id_type=MESH,
        )

    def third(s):
        f = jnp.concatenate([end_straight(s, 0), end_straight(s, 1)], axis=0)
        f = jnp.concatenate([f[: NZ * R], f[NZ * R :]], axis=1)

        @pl.when(lax.rem(s, 2) == 0)
        def _():
            f_even[...] = f

        @pl.when(lax.rem(s, 2) == 1)
        def _():
            p = s // 2
            e = f_even[...]
            low = (lax.broadcasted_iota(jnp.int32, f.shape, 0) % 8) < 4
            z_even = jnp.where(low, e, pltpu.roll(f, 4, 0)).reshape(NZ // 2, 8, WIDE)
            z_odd = jnp.where(low, pltpu.roll(e, NZ * R - 4, 0), f).reshape(NZ // 2, 8, WIDE)
            for i in range(NZ // 2):
                z_send[p, 2 * i] = z_even[i]
                z_send[p, 2 * i + 1] = z_odd[i]
            pltpu.make_async_copy(z_send.at[p, z], z_recv.at[p, z], z_rsem.at[p]).start()
            for d in (4, 3, 5, 2, 6, 1, 7):
                z_copy(p, d).start()

    def last(p):
        pltpu.make_async_copy(z_recv.at[p], z_recv.at[p], z_rsem.at[p]).wait()
        total = z_recv[p, 0]
        for i in range(1, NZ):
            total = total + z_recv[p, i]
        for i in range(2 * R):
            cycle[i // R, i % R, pl.ds(p, 1)] = total[i : i + 1]

    first_row = (rep * GRP + grp) * R
    irrep = lax.broadcasted_iota(jnp.int32, (NIRR, COLS), 0)
    for r in range(R):
        gap = jnp.zeros((NIRR, COLS), jnp.float32)
        limit = jnp.zeros((NIRR, COLS), jnp.int32)
        for s in range(NIRR):
            gap = jnp.where(irrep == s, row_gap[r, s], gap)
            limit = jnp.where(irrep == s, jnp.where(first_row + r < row_count[s], col_count[s], 0), limit)
        gaps[r] = gap + col_gap[...]
        limits[r] = limit

    prepare(0)
    pl.semaphore_wait(barrier, GRP + 3)
    for s in range(AHEAD):
        exchange(s)

    def step(t, _):
        @pl.when(t + AHEAD < NST)
        def _():
            exchange(t + AHEAD)

        @pl.when(t < NST)
        def _():
            multiply(t)

        @pl.when((t >= LAG_M) & (t < NST + LAG_M))
        def _():
            middle(t - LAG_M, 0)
            middle(t - LAG_M, 1)

        @pl.when((t >= LAG_S) & (t < NST + LAG_S))
        def _():
            second(t - LAG_S)

        @pl.when((t >= LAG_T) & (t < NST + LAG_T))
        def _():
            third(t - LAG_T)

        @pl.when((t < NST - 1) & (lax.rem(t, 2) == 1))
        def _():
            prepare((t + 1) // 2)

        @pl.when(t < NST)
        def _():
            first(t)

        @pl.when((t >= LAG_Z) & (lax.rem(t - LAG_Z, 2) == 1))
        def _():
            last((t - LAG_Z) // 2)

        return 0

    lax.fori_loop(0, NST + LAG_Z, step, 0)

    lane = lax.broadcasted_iota(jnp.int32, (NIRR, 128), 1)
    for r in range(R):
        for q in range(COLS // 128):
            total = jnp.zeros((NIRR, 128), jnp.float32)
            for h in range(2):
                part = cycle[h, r, :, 128 * (q // 2) : 128 * (q // 2) + 128]
                for g in range(8):
                    at = 16 * g + CB * h
                    moved = pltpu.roll(part, (at - 64 * (q % 2) - CB * g) % 128, 1)
                    total = jnp.where((lane >= at) & (lane < at + CB), moved, total)
            here = slice(128 * q, 128 * q + 128)
            value = -(total + residual[r, :, here]) / gaps[r, :, here]
            out[r, :, here] = jnp.where(lane + 128 * q < limits[r, :, here], value, 0.0)

    def drain(s, _):
        most = blocks.at[s, pl.ds(0, WIDE - CB)]
        pltpu.make_async_copy(most, most, x_ssem.at[s]).wait()
        core_copy(s).wait_send()
        for ph in range(2):
            for d in (0, 1):
                copy_1(s, ph, d).wait_send()
                both_2(s, ph, d).wait_send()
            for d in (1, 2, 3):
                copy_straight(s, ph, d).wait_send()
        return 0

    lax.fori_loop(0, NST, drain, 0)
    for p in range(NIRR):
        most = z_send.at[p, pl.ds(0, NZ - 1)]
        pltpu.make_async_copy(most, most, z_ssem.at[p]).wait()


def local(amps, integrals, residual_other, row_gap, col_gap, row_count, k_count, col_count):
    f32 = jnp.float32
    vmem, smem = pl.BlockSpec(memory_space=pltpu.VMEM), pl.BlockSpec(memory_space=pltpu.SMEM)
    return pl.pallas_call(
        kernel,
        out_shape=jax.ShapeDtypeStruct((R, NIRR, COLS), f32),
        in_specs=[pl.BlockSpec(memory_space=pl.ANY), pl.BlockSpec(memory_space=pl.ANY), vmem, vmem, smem, smem, smem, smem],
        out_specs=vmem,
        scratch_shapes=[
            pltpu.VMEM((NIRR, ROWS, KB), f32),
            pltpu.VMEM((NST, WIDE, KB), f32),
            pltpu.VMEM((ROWS, 2 * KB), jnp.bfloat16),
            pltpu.VMEM((2, WIDE, 2 * KB), jnp.bfloat16),
            pltpu.VMEM((NST, HALF, WIDE), f32),
            pltpu.VMEM((NST, HALF, WIDE), f32),
            pltpu.VMEM((HALF, WIDE), f32),
            pltpu.VMEM((NST, 4, 2, NX * PR // 2, LANES), f32),
            pltpu.VMEM((NST, 2, NX * PR // 2, LANES), f32),
            pltpu.VMEM((NST, 2, 2, NX * PR // 2, LANES), f32),
            pltpu.VMEM((NST, NX, PR, LANES), f32),
            pltpu.VMEM((NST, 3, PR, LANES), f32),
            pltpu.VMEM((NST, 4, 2, NY * QR // 2, LANES), f32),
            pltpu.VMEM((NST, 2, NY * QR // 2, LANES), f32),
            pltpu.VMEM((NST, 2, 2, NY * QR // 2, LANES), f32),
            pltpu.VMEM((NST, NY, QR, LANES), f32),
            pltpu.VMEM((NST, 3, QR, LANES), f32),
            pltpu.VMEM((NZ * R, WIDE), f32),
            pltpu.VMEM((NIRR, NZ, 2 * R, WIDE), f32),
            pltpu.VMEM((NIRR, NZ, 2 * R, WIDE), f32),
            pltpu.VMEM((R, NIRR, COLS), f32),
            pltpu.VMEM((R, NIRR, COLS), jnp.int32),
            pltpu.VMEM((2, R, NIRR, WIDE), f32),
            pltpu.SemaphoreType.DMA((NIRR,)),
            pltpu.SemaphoreType.DMA((NST,)),
            pltpu.SemaphoreType.DMA((NST,)),
            pltpu.SemaphoreType.DMA((NST,)),
            pltpu.SemaphoreType.DMA((NST,)),
            pltpu.SemaphoreType.DMA((NST, 8)),
            pltpu.SemaphoreType.DMA((NST, 8)),
            pltpu.SemaphoreType.DMA((NST, 6)),
            pltpu.SemaphoreType.DMA((NST, 6)),
            pltpu.SemaphoreType.DMA((NIRR,)),
            pltpu.SemaphoreType.DMA((NIRR,)),
        ],
        compiler_params=pltpu.CompilerParams(
            collective_id=0, has_side_effects=True, vmem_limit_bytes=56 * 2**20
        ),
        cost_estimate=pl.CostEstimate(
            flops=2 * NIRR * ROWS * COLS * KB * 4, bytes_accessed=6 * 2**20, transcendentals=0
        ),
    )(amps, jnp.swapaxes(integrals, 1, 2).reshape(NIRR, 2, CB, -1), residual_other, col_gap, row_gap, row_count, k_count, col_count)


def solution(mesh):
    return jax.shard_map(
        local,
        mesh=mesh,
        in_specs=(
            P(None, None, ("rep", "grp")),
            P(None, "rep", "grp"),
            P(("rep", "grp"), None, None),
            P(("rep", "grp"), None),
            P(),
            P(),
            P(),
            P(),
        ),
        out_specs=P(("rep", "grp"), None, None),
        check_vma=False,
    )
```

time: 124 us -> 97 us (0.78)
  Pallas kernels: 119 us -> 94.6 us
  other arithmetic: 2.17 us -> 0 us
    pallas_call x1, Pallas kernels: 119 us -> 94.6 us  [local(): pl.pallas_call(kernel, out_shape=jax.ShapeDtypeStruct((R, NIRR, COLS), f3...]
    unnamed x6 -> x1, local copies, waits for them, and re-layouts: 0.01 us -> 1.47 us
    lt x2 -> x0, other arithmetic: 1.45 us -> none  [the longest x1 0.73 us: local(): col_index < col_count[None, :, None]]
where the time goes in v2:
time: 97 us; the launch traced here: 96 us
  Pallas kernels  94.6 us (98%)
  local copies, waits for them, and re-layouts  1.47 us (2%)
    pallas_call x1, Pallas kernels, local(): pl.pallas_call(kernel, out_shape=jax.ShapeDtypeStruct((R, NIRR, COLS), f3...  94.6 us

profile of v2, /device:TPU:0, one launch (start us, length us, event | category | flops | bytes accessed | tf_op | source)
XLA Modules:
  0.0 96.0 jit_solution(15779433932186516881)
XLA Ops:
  0.0 94.6 %shard_map.82 = f32[4,8,512]{2,1,0:T(8,128)} custom-call(f32[8,1024,128]{2,1,0:T(8,128)} %amps.1, f32[8,2,8,4096]{3,2,1,0:T(8,128)} %bitcast.3, f32[4,8,512]{2,1,0:T(8,128)} %residual.1, f32[8,512]{1,0:T(8,128)} %col_gap.1, f32[4,8]{1,0:T(4,128)} %row_gap.1, s32[8]{0:T(128)} %row_count.1, s32[8]{0:T(128)} %k_count.1, s32[8]{0:T(128)} %col_count.1), custom_call_target="tpu_custom_call" | custom-call | flops 4294967296 | bytes 6291456 | tf_op jit(solution)/shard_map/pallas_call | solution.py:372
  94.6 1.5 %copy.10 = f32[4,8,512]{2,1,0:T(8,128)} copy(f32[4,8,512]{2,1,0:T(8,128)} %shard_map.82) | data formatting | bytes 131072

commit v3 on v2

--- a/solution.py
+++ b/solution.py
@@ -19,19 +19,20 @@
 WIDE = GRP * CB
 LANES = 128
 UNITS = NZ * R * (WIDE // LANES)
-PR = 40
+PR = 48
 QR = UNITS - PR
 AHEAD = 6
-LAG_M, LAG_S, LAG_T, LAG_Z = 2, 4, 6, 8
+LAG_M, LAG_S, LAG_T = 2, 4, 6
+HELD = (NST - LAG_T) // 2
 
 
 def kernel(
-    amps, ints, residual, col_gap, row_gap, row_count, k_count, col_count, out,
-    left, blocks, lhs, rhs, c_send, c_recv, c_mine,
+    amps, ints, residual_in, col_gap_in, row_gap, row_count, k_count, col_count, out,
+    residual, col_gap, left, blocks, lhs, rhs, c_send, c_recv, c_mine,
     py_d, py_1, py_2, px_d, px_r,
     qx_d, qx_1, qx_2, qy_d, qy_r,
     f_even, z_send, z_recv, gaps, limits, cycle,
-    a_sem, x_ssem, x_rsem, c_ssem, c_rsem, p_ssem, p_rsem, d_ssem, d_rsem, z_ssem, z_rsem,
+    i_sem, a_sem, x_ssem, x_rsem, c_ssem, c_rsem, p_ssem, p_rsem, d_ssem, d_rsem, z_ssem, z_rsem,
 ):
     rep, grp = lax.axis_index("rep"), lax.axis_index("grp")
     y, c = rep // NC, rep % NC
@@ -61,6 +62,12 @@
 
     for s in range(NIRR):
         load(s).start()
+    inputs = (
+        pltpu.make_async_copy(col_gap_in, col_gap, i_sem.at[0]),
+        pltpu.make_async_copy(residual_in, residual, i_sem.at[1]),
+    )
+    for copy in inputs:
+        copy.start()
     barrier = pltpu.get_barrier_semaphore()
 
     def greet(d, _):
@@ -268,18 +275,31 @@
             for i in range(NZ // 2):
                 z_send[p, 2 * i] = z_even[i]
                 z_send[p, 2 * i + 1] = z_odd[i]
-            pltpu.make_async_copy(z_send.at[p, z], z_recv.at[p, z], z_rsem.at[p]).start()
-            for d in (4, 3, 5, 2, 6, 1, 7):
-                z_copy(p, d).start()
+
+    def spread(p):
+        pltpu.make_async_copy(z_send.at[p, z], z_recv.at[p, z], z_rsem.at[p]).start()
+        for d in (4, 3, 5, 2, 6, 1, 7):
+            z_copy(p, d).start()
+
+    lane = lax.broadcasted_iota(jnp.int32, (2 * R, LANES), 1)
 
     def last(p):
         pltpu.make_async_copy(z_recv.at[p], z_recv.at[p], z_rsem.at[p]).wait()
         total = z_recv[p, 0]
         for i in range(1, NZ):
             total = total + z_recv[p, i]
-        for i in range(2 * R):
-            cycle[i // R, i % R, pl.ds(p, 1)] = total[i : i + 1]
-
+        for q in range(COLS // LANES):
+            part = total[:, LANES * (q // 2) : LANES * (q // 2 + 1)]
+            both = jnp.zeros((2 * R, LANES), jnp.float32)
+            for k in range(9):
+                moved = pltpu.roll(part, (CB * k - 64 * (q % 2)) % LANES, 1)
+                both = jnp.where((lane >= 16 * k - CB) & (lane < 16 * k + CB), moved, both)
+            rows = jnp.where(lane % 16 < CB, both, pltpu.roll(both, R, 0))
+            for r in range(R):
+                cycle[r, p : p + 1, LANES * q : LANES * (q + 1)] = rows[r : r + 1]
+
+    for copy in inputs:
+        copy.wait()
     first_row = (rep * GRP + grp) * R
     irrep = lax.broadcasted_iota(jnp.int32, (NIRR, COLS), 0)
     for r in range(R):
@@ -314,10 +334,19 @@
         def _():
             second(t - LAG_S)
 
-        @pl.when((t >= LAG_T) & (t < NST + LAG_T))
+        @pl.when(t == NST)
+        def _():
+            for p in range(HELD):
+                spread(p)
+
+        @pl.when(t >= LAG_T)
         def _():
             third(t - LAG_T)
 
+        @pl.when((t >= LAG_T + 2 * HELD) & (lax.rem(t - LAG_T, 2) == 1))
+        def _():
+            spread((t - LAG_T) // 2)
+
         @pl.when((t < NST - 1) & (lax.rem(t, 2) == 1))
         def _():
             prepare((t + 1) // 2)
@@ -326,27 +355,15 @@
         def _():
             first(t)
 
-        @pl.when((t >= LAG_Z) & (lax.rem(t - LAG_Z, 2) == 1))
-        def _():
-            last((t - LAG_Z) // 2)
-
         return 0
 
-    lax.fori_loop(0, NST + LAG_Z, step, 0)
-
-    lane = lax.broadcasted_iota(jnp.int32, (NIRR, 128), 1)
+    lax.fori_loop(0, NST + LAG_T, step, 0)
+    for p in range(NIRR):
+        last(p)
+
+    column = lax.broadcasted_iota(jnp.int32, (NIRR, COLS), 1)
     for r in range(R):
-        for q in range(COLS // 128):
-            total = jnp.zeros((NIRR, 128), jnp.float32)
-            for h in range(2):
-                part = cycle[h, r, :, 128 * (q // 2) : 128 * (q // 2) + 128]
-                for g in range(8):
-                    at = 16 * g + CB * h
-                    moved = pltpu.roll(part, (at - 64 * (q % 2) - CB * g) % 128, 1)
-                    total = jnp.where((lane >= at) & (lane < at + CB), moved, total)
-            here = slice(128 * q, 128 * q + 128)
-            value = -(total + residual[r, :, here]) / gaps[r, :, here]
-            out[r, :, here] = jnp.where(lane + 128 * q < limits[r, :, here], value, 0.0)
+        out[r] = jnp.where(column < limits[r], -(cycle[r] + residual[r]) / gaps[r], 0.0)
 
     def drain(s, _):
         most = blocks.at[s, pl.ds(0, WIDE - CB)]
@@ -368,13 +385,16 @@
 
 def local(amps, integrals, residual_other, row_gap, col_gap, row_count, k_count, col_count):
     f32 = jnp.float32
+    hbm = pl.BlockSpec(memory_space=pl.ANY)
     vmem, smem = pl.BlockSpec(memory_space=pltpu.VMEM), pl.BlockSpec(memory_space=pltpu.SMEM)
     return pl.pallas_call(
         kernel,
         out_shape=jax.ShapeDtypeStruct((R, NIRR, COLS), f32),
-        in_specs=[pl.BlockSpec(memory_space=pl.ANY), pl.BlockSpec(memory_space=pl.ANY), vmem, vmem, smem, smem, smem, smem],
+        in_specs=[hbm, hbm, hbm, hbm, smem, smem, smem, smem],
         out_specs=vmem,
         scratch_shapes=[
+            pltpu.VMEM((R, NIRR, COLS), f32),
+            pltpu.VMEM((NIRR, COLS), f32),
             pltpu.VMEM((NIRR, ROWS, KB), f32),
             pltpu.VMEM((NST, WIDE, KB), f32),
             pltpu.VMEM((ROWS, 2 * KB), jnp.bfloat16),
@@ -397,7 +417,8 @@
             pltpu.VMEM((NIRR, NZ, 2 * R, WIDE), f32),
             pltpu.VMEM((R, NIRR, COLS), f32),
             pltpu.VMEM((R, NIRR, COLS), jnp.int32),
-            pltpu.VMEM((2, R, NIRR, WIDE), f32),
+            pltpu.VMEM((R, NIRR, COLS), f32),
+            pltpu.SemaphoreType.DMA((2,)),
             pltpu.SemaphoreType.DMA((NIRR,)),
             pltpu.SemaphoreType.DMA((NST,)),
             pltpu.SemaphoreType.DMA((NST,)),

time: 97 us -> 96.7 us (level)
  no operation moved by 1% of the time
where the time goes in v3:
time: 96.7 us; the launch traced here: 95.4 us
  Pallas kernels  93.9 us (97%)
  local copies, waits for them, and re-layouts  1.47 us (2%)
    pallas_call x1, Pallas kernels, local(): pl.pallas_call(kernel, out_shape=jax.ShapeDtypeStruct((R, NIRR, COLS), f3...  93.9 us

profile of v3, /device:TPU:0, one launch (start us, length us, event | category | flops | bytes accessed | tf_op | source)
XLA Modules:
  0.0 95.4 jit_solution(12701274093386235161)
XLA Ops:
  0.0 93.9 %shard_map.82 = f32[4,8,512]{2,1,0:T(8,128)} custom-call(f32[8,1024,128]{2,1,0:T(8,128)} %amps.1, f32[8,2,8,4096]{3,2,1,0:T(8,128)} %bitcast.3, f32[4,8,512]{2,1,0:T(8,128)} %residual_in.1, f32[8,512]{1,0:T(8,128)} %col_gap_in.1, f32[4,8]{1,0:T(4,128)} %row_gap.1, s32[8]{0:T(128)} %row_count.1, s32[8]{0:T(128)} %k_count.1, s32[8]{0:T(128)} %col_count.1), custom_call_target="tpu_custom_call" | custom-call | flops 4294967296 | bytes 6291456 | tf_op jit(solution)/shard_map/pallas_call | solution.py:390
  93.9 1.5 %copy.10 = f32[4,8,512]{2,1,0:T(8,128)} copy(f32[4,8,512]{2,1,0:T(8,128)} %shard_map.82) | data formatting | bytes 131072

commit v4 on v3

--- a/solution.py
+++ b/solution.py
@@ -183,9 +183,9 @@
             copy_straight(s, ph, d).wait_recv()
         return data[s, me] + got[s, 0] + got[s, 1] + got[s, 2]
 
-    def core_copy(s):
-        return pltpu.make_async_remote_copy(
-            c_send.at[s], c_recv.at[s], c_ssem.at[s], c_rsem.at[s], device_id=sibling, device_id_type=MESH
+    def core_copy(s, i):
+        return pltpu.make_async_remote_copy(
+            c_send.at[s, i], c_recv.at[s, i], c_ssem.at[s, i], c_rsem.at[s, i], device_id=sibling, device_id_type=MESH
         )
 
     def prepare(s):
@@ -211,8 +211,9 @@
 
         lax.fori_loop(0, NY * NC, block, 0)
 
-    def product(half):
-        rows = lhs[pl.ds(pl.multiple_of(half * HALF, HALF), HALF)]
+    def product(half, i):
+        part = HALF // 2
+        rows = lhs[pl.ds(pl.multiple_of(half * HALF + i * part, part), part)]
         dims = (((1,), (1,)), ((), ()))
         return lax.dot_general(rows, rhs[0], dims, preferred_element_type=jnp.float32) + lax.dot_general(
             rows, rhs[1], dims, preferred_element_type=jnp.float32
@@ -226,12 +227,15 @@
         lo = (b - hi.astype(jnp.float32)).astype(jnp.bfloat16)
         rhs[0] = jnp.concatenate([hi, hi], axis=1)
         rhs[1] = jnp.concatenate([lo, lo], axis=1)
-        c_send[s] = product(1 - c)
-        core_copy(s).start()
-        c_mine[...] = product(c)
+        for i in (0, 1):
+            c_send[s, i] = product(1 - c, i)
+            core_copy(s, i).start()
+        for i in (0, 1):
+            c_mine[i] = product(c, i)
 
     def first(s):
-        core_copy(s).wait_recv()
+        for i in (0, 1):
+            core_copy(s, i).wait_recv()
         total = (c_mine[...] + c_recv[s]).reshape(NY, NX, NZ * R, WIDE)
         total = jnp.concatenate([total[..., :LANES], total[..., LANES:]], axis=2)
         py_d[s] = total[:, :, :PR].reshape(NY, 2, NX * PR // 2, LANES)
@@ -368,7 +372,8 @@
     def drain(s, _):
         most = blocks.at[s, pl.ds(0, WIDE - CB)]
         pltpu.make_async_copy(most, most, x_ssem.at[s]).wait()
-        core_copy(s).wait_send()
+        for i in (0, 1):
+            core_copy(s, i).wait_send()
         for ph in range(2):
             for d in (0, 1):
                 copy_1(s, ph, d).wait_send()
@@ -399,9 +404,9 @@
             pltpu.VMEM((NST, WIDE, KB), f32),
             pltpu.VMEM((ROWS, 2 * KB), jnp.bfloat16),
             pltpu.VMEM((2, WIDE, 2 * KB), jnp.bfloat16),
-            pltpu.VMEM((NST, HALF, WIDE), f32),
-            pltpu.VMEM((NST, HALF, WIDE), f32),
-            pltpu.VMEM((HALF, WIDE), f32),
+            pltpu.VMEM((NST, 2, HALF // 2, WIDE), f32),
+            pltpu.VMEM((NST, 2, HALF // 2, WIDE), f32),
+            pltpu.VMEM((2, HALF // 2, WIDE), f32),
             pltpu.VMEM((NST, 4, 2, NX * PR // 2, LANES), f32),
             pltpu.VMEM((NST, 2, NX * PR // 2, LANES), f32),
             pltpu.VMEM((NST, 2, 2, NX * PR // 2, LANES), f32),
@@ -422,8 +427,8 @@
             pltpu.SemaphoreType.DMA((NIRR,)),
             pltpu.SemaphoreType.DMA((NST,)),
             pltpu.SemaphoreType.DMA((NST,)),
-            pltpu.SemaphoreType.DMA((NST,)),
-            pltpu.SemaphoreType.DMA((NST,)),
+            pltpu.SemaphoreType.DMA((NST, 2)),
+            pltpu.SemaphoreType.DMA((NST, 2)),
             pltpu.SemaphoreType.DMA((NST, 8)),
             pltpu.SemaphoreType.DMA((NST, 8)),
             pltpu.SemaphoreType.DMA((NST, 6)),

time: 96.7 us -> 96.5 us (level)
  no operation moved by 1% of the time
where the time goes in v4:
time: 96.5 us; the launch traced here: 95.1 us
  Pallas kernels  93.7 us (97%)
  local copies, waits for them, and re-layouts  1.47 us (2%)
    pallas_call x1, Pallas kernels, local(): pl.pallas_call(kernel, out_shape=jax.ShapeDtypeStruct((R, NIRR, COLS), f3...  93.7 us

profile of v4, /device:TPU:0, one launch (start us, length us, event | category | flops | bytes accessed | tf_op | source)
XLA Modules:
  0.0 95.1 jit_solution(4016043665209398320)
XLA Ops:
  0.0 93.7 %shard_map.82 = f32[4,8,512]{2,1,0:T(8,128)} custom-call(f32[8,1024,128]{2,1,0:T(8,128)} %amps.1, f32[8,2,8,4096]{3,2,1,0:T(8,128)} %bitcast.3, f32[4,8,512]{2,1,0:T(8,128)} %residual_in.1, f32[8,512]{1,0:T(8,128)} %col_gap_in.1, f32[4,8]{1,0:T(4,128)} %row_gap.1, s32[8]{0:T(128)} %row_count.1, s32[8]{0:T(128)} %k_count.1, s32[8]{0:T(128)} %col_count.1), custom_call_target="tpu_custom_call" | custom-call | flops 4294967296 | bytes 6291456 | tf_op jit(solution)/shard_map/pallas_call | solution.py:395
  93.7 1.5 %copy.10 = f32[4,8,512]{2,1,0:T(8,128)} copy(f32[4,8,512]{2,1,0:T(8,128)} %shard_map.82) | data formatting | bytes 131072
